TPU v7x, 32 devices: a whole 2x2x4 slice. The times are simulated.
32 devices in a mesh: req: 16 (over z, x, core), mdl: 2 (over y).
Axes of the slice: x: 2, y: 2, z: 4, core: 2. Of those that a mesh axis runs over, the one named last changes fastest.
Arguments:
- hidden: bfloat16 [4096, 1536], P(('req', 'mdl')), may hold values from -6 to 6
- input_gain: float32 [1536], replicated, may hold values from 0.1 to 1.9
- gate_proj: bfloat16 [1536, 3072], P('req', 'mdl'), may hold values from -0.15625 to 0.15625
- value_proj: bfloat16 [1536, 3072], P('req', 'mdl'), may hold values from -0.15625 to 0.15625
- state_proj: bfloat16 [1536, 256], P('req'), may hold values from -0.15625 to 0.15625
- step_proj: bfloat16 [1536, 48], P('req', 'mdl'), may hold values from -0.15625 to 0.15625
- conv_value: float32 [5, 3072], P(None, 'mdl'), may hold values from -3 to 3
- conv_state: float32 [5, 256], replicated, may hold values from -3 to 3
- step_bias: float32 [48], P('mdl'), may hold values from -4 to -1
- decay_log: float32 [48], P('mdl'), may hold values from -4 to 0
- skip_gain: float32 [48], P('mdl'), may hold values from 0.5 to 1.5
- output_gain: float32 [3072], P('mdl'), may hold values from 0.1 to 1.9
- out_proj: bfloat16 [3072, 1536], P('mdl', 'req'), may hold values from -0.109375 to 0.109375
- state_start: float32 [32, 48, 64, 128], P('req', 'mdl'), may hold values from -0.8 to 0.8
- edge_value: bfloat16 [32, 3, 3072], P('req', None, 'mdl'), may hold values from -6 to 6
- edge_state: bfloat16 [32, 3, 256], P('req'), may hold values from -6 to 6
- lengths: int32 [32], P('req'), may hold values from 1 to 128, as said below
- accepted: int32 [32], P('req'), may hold values from 1 to 128, as said below
Outputs:
- mixed: bfloat16 [4096, 1536], P(('req', 'mdl'))
- state_final: float32 [32, 48, 64, 128], P(('req', 'mdl'))
- edge_final: bfloat16 [32, 3, 3328], P(('req', 'mdl'))
Inputs may be any that keep to these rules, and one draw needn't show every extreme that they name: `lengths`: one request's draft fills all 128 slots. accepted[r] <= lengths[r]; the request whose draft fills all slots accepts all of it.
All inputs are finite; a program needn't handle non-finite values.
Results may differ from a plain program's by a relative error of at most 0.009.
Values may be sent and summed in bfloat16 or wider, within the bound.
A program may use at most 64 MiB of HBM per device.

v0:
```python
import jax
import jax.numpy as jnp
from jax import lax
from jax.sharding import PartitionSpec as P

EPSILON = 1e-05
HIGHEST = lax.Precision.HIGHEST


def local(
    hidden,
    input_gain,
    gate_proj,
    value_proj,
    state_proj,
    step_proj,
    conv_value,
    conv_state,
    step_bias,
    decay_log,
    skip_gain,
    output_gain,
    out_proj,
    state_start,
    edge_value,
    edge_state,
    lengths,
    accepted,
):
    requests, heads_here, head_dim, nstate = state_start.shape
    rows_dev = hidden.shape[0]
    span = rows_dev * lax.axis_size("mdl") // requests
    here_count = rows_dev // span
    group_rows = requests * span
    inner_here = heads_here * head_dim
    width_k = conv_value.shape[0] - 1
    edge_count = width_k - 1
    my_index = lax.axis_index("mdl")
    floats = hidden.astype(jnp.float32)
    normed = (
        floats * lax.rsqrt(jnp.mean(floats * floats, -1, keepdims=True) + EPSILON) * input_gain
    ).astype(jnp.bfloat16)
    widths = (gate_proj.shape[1], value_proj.shape[1], state_proj.shape[1], step_proj.shape[1])
    first_end = widths[0]
    second_end = first_end + widths[1]
    third_end = second_end + widths[2]
    whole = lax.all_gather(normed, "mdl", axis=0, tiled=True)
    packed = jnp.concatenate((gate_proj, value_proj, state_proj, step_proj), 1)
    joined_piece = lax.all_gather(packed, "req", axis=0, tiled=True)
    joined = jnp.dot(whole, joined_piece, preferred_element_type=jnp.float32)
    gates = joined[:, :first_end].astype(jnp.bfloat16)
    values = joined[:, first_end:second_end].astype(jnp.bfloat16)
    readers = joined[:, second_end:third_end].astype(jnp.bfloat16)
    step_raw = joined[:, third_end:].astype(jnp.bfloat16)
    current = jnp.concatenate([values, readers], 1).reshape(requests, span, -1)
    edges = jnp.concatenate([edge_value, edge_state], 2)
    extended = jnp.concatenate([edges, current], 1).astype(jnp.float32)
    taps = jnp.concatenate([conv_value, conv_state], 1)
    convolved = taps[width_k][None, None, :] + jnp.zeros(
        (requests, span, taps.shape[1]), jnp.float32
    )
    for shift in range(width_k):
        convolved = convolved + taps[shift][None, None, :] * extended[:, shift : shift + span]
    active = jax.nn.silu(convolved).astype(jnp.bfloat16)
    vals = active[..., :inner_here].reshape(requests, span, heads_here, head_dim)
    inputs_b = active[..., inner_here : inner_here + nstate]
    reads_c = active[..., inner_here + nstate :]
    vals_f = vals.astype(jnp.float32)
    steps = jax.nn.softplus(
        step_raw.astype(jnp.float32).reshape(requests, span, heads_here) + step_bias
    )
    logs = -steps * jnp.exp(decay_log)
    sooner = jnp.arange(span, dtype=jnp.int32)
    triangle = (sooner[:, None] >= sooner[None, :]).astype(jnp.float32)
    running = jnp.einsum("ts,gsh->gth", triangle, logs, precision=HIGHEST)
    intersection = jnp.einsum("gtn,gsn->gts", reads_c, inputs_b, preferred_element_type=jnp.float32)
    positions = jnp.arange(span, dtype=jnp.int32)
    lower = positions[:, None] >= positions[None, :]
    spread = jnp.where(
        lower[None, :, :, None], running[:, :, None, :] - running[:, None, :, :], -jnp.inf
    )
    kernel = intersection[..., None] * jnp.exp(spread) * steps[:, None, :, :]
    outputs = jnp.einsum("gtsh,gshp->gthp", kernel, vals_f, precision=HIGHEST)
    carried = jnp.einsum(
        "gtn,ghpn->gthp", reads_c.astype(jnp.float32), state_start, precision=HIGHEST
    )
    outputs = outputs + jnp.exp(running)[..., None] * carried + skip_gain[:, None] * vals_f
    product = outputs.reshape(group_rows, inner_here) * jax.nn.silu(gates.astype(jnp.float32))
    squares = jnp.sum(product * product, -1)
    gated = (product * output_gain).astype(jnp.bfloat16)
    total_squares = lax.psum(squares, "mdl")
    scale = lax.rsqrt(total_squares / (inner_here * lax.axis_size("mdl")) + EPSILON)
    partial_terms = jnp.dot(
        gated,
        lax.all_gather(out_proj, "req", axis=1, tiled=True),
        preferred_element_type=jnp.float32,
    )
    mine = lax.psum_scatter(
        partial_terms.astype(jnp.bfloat16), "mdl", scatter_dimension=0, tiled=True
    ).astype(jnp.float32)
    my_scale = lax.dynamic_slice_in_dim(scale, my_index * rows_dev, rows_dev, 0)
    my_lengths = lax.dynamic_slice_in_dim(lengths, my_index * here_count, here_count, 0)
    live = (positions[None, :] < my_lengths[:, None]).reshape(rows_dev).astype(jnp.float32)
    mixed = (mine * my_scale[:, None] * live[:, None]).astype(jnp.bfloat16)
    last = accepted - 1
    chosen = (positions[None, :] == last[:, None]).astype(jnp.float32)
    running_last = jnp.sum(chosen[:, :, None] * running, axis=1)
    before = positions[None, :] <= last[:, None]
    reach = jnp.where(before[:, :, None], running_last[:, None, :] - running, -jnp.inf)
    weights_s = jnp.exp(reach) * steps
    gathered_state = jnp.einsum(
        "gsh,gshp,gsn->ghpn", weights_s, vals_f, inputs_b.astype(jnp.float32), precision=HIGHEST
    )
    state_here = jnp.exp(running_last)[:, :, None, None] * state_start + gathered_state
    picks = accepted[:, None] + jnp.arange(edge_count, dtype=jnp.int32)[None, :]
    selected = jnp.take_along_axis(extended, picks[:, :, None], axis=1)
    value_edges = selected[..., :inner_here].reshape(requests, edge_count, heads_here, head_dim)
    value_edges = value_edges.transpose(0, 2, 1, 3).reshape(
        requests, heads_here, edge_count * head_dim
    )
    states_home, edges_home = (
        lax.all_to_all(
            state_here.reshape(requests, heads_here, head_dim * nstate).astype(jnp.bfloat16),
            "mdl",
            split_axis=0,
            concat_axis=1,
            tiled=True,
        ).astype(jnp.float32),
        lax.all_to_all(
            value_edges.astype(jnp.bfloat16), "mdl", split_axis=0, concat_axis=1, tiled=True
        ).astype(value_edges.dtype),
    )
    heads_all = states_home.shape[1]
    state_final = states_home.reshape(here_count, heads_all, head_dim, nstate)
    edges_home = edges_home.reshape(here_count, heads_all, edge_count, head_dim).transpose(
        0, 2, 1, 3
    )
    edges_home = edges_home.reshape(here_count, edge_count, heads_all * head_dim)
    state_edges = lax.dynamic_slice_in_dim(
        selected[..., inner_here:], my_index * here_count, here_count, 0
    )
    edge_final = jnp.concatenate([edges_home, state_edges], 2).astype(jnp.bfloat16)
    return (mixed, state_final, edge_final)


def solution(mesh):
    return jax.shard_map(
        local,
        mesh=mesh,
        in_specs=(
            P(("req", "mdl"), None),
            P(),
            P("req", "mdl"),
            P("req", "mdl"),
            P("req", None),
            P("req", "mdl"),
            P(None, "mdl"),
            P(),
            P("mdl"),
            P("mdl"),
            P("mdl"),
            P("mdl"),
            P("mdl", "req"),
            P("req", "mdl", None, None),
            P("req", None, "mdl"),
            P("req", None, None),
            P("req"),
            P("req"),
        ),
        out_specs=(
            P(("req", "mdl"), None),
            P(("req", "mdl"), None, None, None),
            P(("req", "mdl"), None, None),
        ),
        check_vma=False,
    )
```

profile of v0, /device:TPU:0, one launch (start us, length us, event | category | flops | bytes accessed | tf_op | source)
XLA Modules:
  0.0 201.5 jit_solution(17263862476050745246)
XLA Ops:
  7.3 0.9 copy.52
  8.2 2.0 pad_maximum_fusion
  10.2 0.7 all-gather.5.cloned.1.call-update
  11.1 0.1 fusion.43
  11.1 0.1 reshape.272
  11.2 0.6 dynamic_slice.10
  11.8 0.6 compare_convert_fusion.1
  12.5 0.1 slice_reduce_fusion.4
  12.6 0.2 fusion.24
  12.8 0.2 fusion.26
  13.0 12.8 %all_gather.9 = bf16[256,1536]{1,0:T(8,128)(2,1)S(1)} all-gather(bf16[128,1536]{1,0:T(8,128)(2,1)S(1)} %fusion.26), channel_id=1, replica_groups=mesh['req'=16,'mdl'=2] {'mdl'}, dimensions={0}, use_global_device_ids=true | all-gather | bytes 1179648 | tf_op jit(solution)/shard_map/all_gather | solution.py:47
  25.8 0.1 compare_and_fusion
  25.8 0.1 iota_compare_fusion.2
  25.9 76.5 %all-gather.3.cloned.1.call-done = bf16[1536,3352]{1,0:T(8,128)(2,1)} async-done(((bf16[96,3352]{1,0:T(8,128)(2,1)}), bf16[1536,3352]{1,0:T(8,128)(2,1)}) %all-gather.3.cloned.1.call-update) | async-done | bytes 10297360 | tf_op jit(solution)/shard_map/all_gather | solution.py:49
  102.4 8.3 %convolution_convert_fusion = bf16[256,3352]{0,1:T(8,128)(2,1)S(1)} fusion(bf16[256,1536]{1,0:T(8,128)(2,1)S(1)} %all_gather.9, bf16[1536,3352]{1,0:T(8,128)(2,1)} %all-gather.3.cloned.1.call-done), kind=kOutput, calls=%fused_computation.1 | convolution fusion | flops 2636978176 | bytes 12800000 | tf_op jit(solution)/shard_map/dot_general | solution.py:50
  110.7 1.2 copy-done.3
  111.9 0.8 copy.63
  112.7 0.2 maximum_convert_fusion
  112.9 1.9 copy.57
  114.8 1.2 multiply_convert_fusion
  116.1 1.2 copy.54
  117.3 0.8 compare_select_fusion
  118.1 1.0 multiply_reduce_fusion.1
  119.1 0.8 exponential_multiply_fusion
  119.9 0.2 fusion.34
  120.1 0.8 fusion.30
  121.0 0.1 copy-done.2
  121.1 3.5 %fusion.10 = f32[2,128,24,64]{1,3,2,0:T(8,128)S(1)} fusion(bf16[2,128,24,64]{1,3,2,0:T(8,128)(2,1)S(1)} %bitcast.75, f32[2,128,24,64]{1,3,2,0:T(8,128)S(1)} %fusion.30, f32[2,128,24]{1,2,0:T(8,128)S(1)} %compare_select_fusion, f32[2,128,24]{1,2,0:T(8,128)S(1)} %get-tuple-element.13, f32[2,128,128]{2,1,0:T(8,128)S(1)} %fusion.34, ...), kind=kOutput, calls=%fused_computation.22 | convolution fusion | flops 609091584 | bytes 4153440 | tf_op jit(solution)/shard_map/gtsh,gshp->gthp/dot_general | solution.py:83
  124.6 1.2 copy.56
  125.8 30.4 %all-gather.5.cloned.1.call-done = bf16[1536,1536]{0,1:T(8,128)(2,1)} async-done(((bf16[1536,96]{0,1:T(8,128)(2,1)}), bf16[1536,1536]{0,1:T(8,128)(2,1)}) %all-gather.5.cloned.1.call-update) | async-done | bytes 4718608 | tf_op jit(solution)/shard_map/all_gather | solution.py:95
  156.2 5.3 %convolution_convert_fusion.1 = bf16[256,1536]{1,0:T(8,128)(2,1)} fusion(bf16[1536,1536]{0,1:T(8,128)(2,1)} %all-gather.5.cloned.1.call-done, f32[1536]{0:T(1024)S(1)} %copy-done.11, f32[192,8,2,128]{3,2,1,0:T(2,128)S(1)} %bitcast.71, bf16[256,3352]{0,1:T(8,128)(2,1)} %copy-done.3), kind=kOutput, calls=%fused_computation.8 | convolution fusion | flops 1211498496 | bytes 7870464 | tf_op jit(solution)/shard_map/dot_general | solution.py:93
  161.6 1.4 gather_fusion
  163.0 0.1 broadcast_select_fusion
  163.2 0.1 convert_element_type.121
  163.3 0.7 convert_element_type.123
  164.0 3.3 %all-to-all-start.1 = ((bf16[2,24,192]{2,1,0:T(8,128)(2,1)}), bf16[2,24,192]{2,1,0:T(8,128)(2,1)S(1)}, u32[]{:S(2)}, u32[]{:S(2)}) async-start(bf16[2,24,192]{2,1,0:T(8,128)(2,1)} %convert_element_type.123), calls=%async_computation.2 | async-start | bytes 49152 | tf_op jit(solution)/shard_map/all_to_all | solution.py:129
  167.3 1.7 multiply_reduce_fusion
  168.9 5.0 %psum.7 = f32[256]{0:T(256)S(1)} all-reduce(f32[256]{0:T(256)S(1)} %multiply_reduce_fusion), channel_id=1, replica_groups=mesh['req'=16,'mdl'=2] {'mdl'}, use_global_device_ids=true, to_apply=%region_3.4 | all-reduce | flops 256 | bytes 2048 | tf_op jit(solution)/shard_map/psum | solution.py:91
  173.9 2.1 %add_convert_fusion = bf16[2,24,64,128]{3,2,1,0:T(8,128)(2,1)S(1)} fusion(f32[2,24,64,128]{3,2,1,0:T(8,128)S(1)} %copy-done, bf16[2,128,24,64]{1,3,2,0:T(8,128)(2,1)} %bitcast.74, f32[2,128,24]{1,2,0:T(8,128)S(1)} %get-tuple-element.8, f32[2,24]{1,0:T(2,128)S(1)} %exp.41, bf16[2,128,1792]{2,1,0:T(8,128)(2,1)} %copy-done.1), kind=kOutput, calls=%fused_computation.29 | convolution fusion | flops 605945856 | bytes 3236032 | tf_op jit(solution)/shard_map/gsh,gshp,gsn->ghpn/dot_general | solution.py:111
  176.1 1.2 convert_element_type.118
  177.3 0.1 dynamic_slice.9
  177.4 3.5 %all-to-all-start = ((bf16[2,24,8192]{2,1,0:T(8,128)(2,1)}), bf16[2,24,8192]{2,1,0:T(8,128)(2,1)S(1)}, u32[]{:S(2)}, u32[]{:S(2)}) async-start(bf16[2,24,8192]{2,1,0:T(8,128)(2,1)} %convert_element_type.118), calls=%async_computation.1 | async-start | bytes 1572864 | tf_op jit(solution)/shard_map/all_to_all | solution.py:122
  180.9 0.1 convert_element_type.124
  181.0 0.1 concatenate.34
  181.1 0.6 pad_maximum_fusion.1
  181.8 9.9 %all-to-all-done = bf16[2,24,8192]{2,1,0:T(8,128)(2,1)S(1)} async-done(((bf16[2,24,8192]{2,1,0:T(8,128)(2,1)}), bf16[2,24,8192]{2,1,0:T(8,128)(2,1)S(1)}, u32[]{:S(2)}, u32[]{:S(2)}) %all-to-all-start) | async-done | bytes 786464 | tf_op jit(solution)/shard_map/all_to_all | solution.py:122
  191.7 1.3 copy.66
  193.0 2.0 multiply_convert_fusion.3
  (56 shorter events, 0.5 us)
Async XLA Ops:
  7.2 3.8 %copy-start.6 = (bf16[2,3,1536]{2,0,1:T(2,128)(2,1)S(1)}, bf16[2,3,1536]{2,0,1:T(2,128)(2,1)}, u32[]{:S(2)}) copy-start(bf16[2,3,1536]{2,0,1:T(2,128)(2,1)} %param.32) | copy-start | bytes 55300
  7.2 3.8 %copy-start.9 = (bf16[2,3,256]{2,0,1:T(2,128)(2,1)S(1)}, bf16[2,3,256]{2,0,1:T(2,128)(2,1)}, u32[]{:S(2)}) copy-start(bf16[2,3,256]{2,0,1:T(2,128)(2,1)} %param.33) | copy-start | bytes 9220
  7.2 3.8 %copy-start.12 = (f32[24]{0:T(128)S(1)}, f32[24]{0:T(128)}, u32[]{:S(2)}) copy-start(f32[24]{0:T(128)} %param.27) | copy-start | bytes 292
  7.2 3.9 %copy-start.14 = (s32[2]{0:T(128)S(1)}, s32[2]{0:T(128)}, u32[]{:S(2)}) copy-start(s32[2]{0:T(128)} %param.35) | copy-start | bytes 28
  7.2 4.0 %copy-start.13 = (s32[2]{0:T(128)S(1)}, s32[2]{0:T(128)}, u32[]{:S(2)}) copy-start(s32[2]{0:T(128)} %param.34) | copy-start | bytes 28
  7.2 5.3 %copy-start.5 = (f32[5,1536]{1,0:T(8,128)S(1)}, f32[5,1536]{1,0:T(8,128)}, u32[]{:S(2)}) copy-start(f32[5,1536]{1,0:T(8,128)} %param.24) | copy-start | bytes 92164
  7.2 5.3 %copy-start.8 = (f32[5,256]{1,0:T(8,128)S(1)}, f32[5,256]{1,0:T(8,128)}, u32[]{:S(2)}) copy-start(f32[5,256]{1,0:T(8,128)} %param.25) | copy-start | bytes 15364
  7.2 5.4 %copy-start.4 = (bf16[128,1536]{1,0:T(8,128)(2,1)S(1)}, bf16[128,1536]{1,0:T(8,128)(2,1)}, u32[]{:S(2)}) copy-start(bf16[128,1536]{1,0:T(8,128)(2,1)} %param.18) | copy-start | bytes 1179652
  7.2 5.6 %copy-start.7 = (f32[1536]{0:T(1024)S(1)}, f32[1536]{0:T(1024)}, u32[]{:S(2)}) copy-start(f32[1536]{0:T(1024)} %param.19) | copy-start | bytes 18436
  7.3 95.1 %all-gather.3.cloned.1.call-start = ((), (), s32[]{:S(2)}) async-start(), calls=%async_computation.3 | async-start | bytes 11280384 | tf_op jit(solution)/shard_map/all_gather | solution.py:49
  10.2 146.1 %all-gather.5.cloned.1.call-start = ((), (), s32[]{:S(2)}) async-start(), calls=%async_computation.4 | async-start | bytes 5013504 | tf_op jit(solution)/shard_map/all_gather | solution.py:95
  10.9 182.1 %reduce-scatter.2.cloned.1.call-start = ((), (), s32[]{:S(2)}) async-start(), calls=%async_computation.5 | async-start | bytes 1179648 | tf_op jit(solution)/shard_map/reduce_scatter | solution.py:98
  110.6 1.2 copy-start.3
  116.0 4.1 %copy-start.1 = (bf16[2,128,1792]{2,1,0:T(8,128)(2,1)}, bf16[2,128,1792]{2,1,0:T(8,128)(2,1)S(1)}, u32[]{:S(2)}) copy-start(bf16[2,128,1792]{2,1,0:T(8,128)(2,1)S(1)} %multiply_convert_fusion) | copy-start | bytes 2752516
  116.0 1.3 copy-start.10
  116.0 4.1 %copy-start = (f32[2,24,64,128]{3,2,1,0:T(8,128)S(1)}, f32[2,24,64,128]{3,2,1,0:T(8,128)}, u32[]{:S(2)}) copy-start(f32[2,24,64,128]{3,2,1,0:T(8,128)} %param.31) | copy-start | bytes 4718596
  119.9 1.1 copy-start.2
  119.9 1.1 copy-start.15
  124.6 31.7 %copy-start.11 = (f32[1536]{0:T(1024)S(1)}, f32[1536]{0:T(1024)}, u32[]{:S(2)}) copy-start(f32[1536]{0:T(1024)} %param.29) | copy-start | bytes 18436
  164.0 13.4 %all-to-all-start.1 = ((bf16[2,24,192]{2,1,0:T(8,128)(2,1)}), bf16[2,24,192]{2,1,0:T(8,128)(2,1)S(1)}, u32[]{:S(2)}, u32[]{:S(2)}) async-start(bf16[2,24,192]{2,1,0:T(8,128)(2,1)} %convert_element_type.123), calls=%async_computation.2 | async-start | bytes 49152 | tf_op jit(solution)/shard_map/all_to_all | solution.py:129
  177.4 14.3 %all-to-all-start = ((bf16[2,24,8192]{2,1,0:T(8,128)(2,1)}), bf16[2,24,8192]{2,1,0:T(8,128)(2,1)S(1)}, u32[]{:S(2)}, u32[]{:S(2)}) async-start(bf16[2,24,8192]{2,1,0:T(8,128)(2,1)} %convert_element_type.118), calls=%async_computation.1 | async-start | bytes 1572864 | tf_op jit(solution)/shard_map/all_to_all | solution.py:122
Sparse Core Ops, SparseCore 0:
  10.9 91.3 all-gather.2
  104.6 51.5 all-gather.4
  161.7 16.3 reduce-scatter.1
where the time goes:
time: 202 us
  waiting for transfers between devices  118 us (58%)
  matrix products  21.2 us (10%)
  blocking collectives  17.7 us (9%)
  between operations  14.2 us (7%)
  local copies, waits for them, and re-layouts  13.4 us (7%)
  other arithmetic  10.6 us (5%)
  starting transfers between devices  6.91 us (3%)
    all_gather x1, waiting for transfers between devices, local(): joined_piece = lax.all_gather(packed, 'req', axis=0, tiled=True)  76.5 us
    all_gather x1, waiting for transfers between devices, local(): lax.all_gather(out_proj, 'req', axis=1, tiled=True)  30.4 us
    all_gather x1, blocking collectives, local(): whole = lax.all_gather(normed, 'mdl', axis=0, tiled=True)  12.8 us
    all_to_all x1, waiting for transfers between devices, local(): lax.all_to_all(state_here.reshape(requests, heads_here, head_dim * nstate...  9.9 us
    dot_general x1, matrix products, local(): joined = jnp.dot(whole, joined_piece, preferred_element_type=jnp.float32)  8.28 us
    dot_general x1, matrix products, local(): jnp.dot(gated, lax.all_gather(out_proj, 'req', axis=1, tiled=True), prefe...  5.3 us
    psum x1, blocking collectives, local(): total_squares = lax.psum(squares, 'mdl')  4.99 us
  transfers between devices with their start and end apart: 5, of which 3 were waited for; matrix products, arithmetic and copies ran while one was open for 17% of the time, Pallas kernels for 0%

commit v1 on v0

--- a/solution.py
+++ b/solution.py
@@ -5,6 +5,31 @@
 
 EPSILON = 1e-05
 HIGHEST = lax.Precision.HIGHEST
+
+
+def _define_terms(field, k_dim):
+    odd = list(field.shape[1:])
+    odd[k_dim] *= field.shape[0]
+    return jnp.moveaxis(field, 0, k_dim).reshape(odd)
+
+
+def write_object(u_in, out_dim, along_axis):
+    num = lax.axis_size(along_axis)
+    blocks_here = tuple(((c, (c + 1) % num) for c in range(num)))
+    by_rank = tuple(((to_i, no) for no, to_i in blocks_here))
+    g_now, z2 = ([], [])
+    for jj in range(num - 1):
+        if jj % 2 == 0:
+            z = lax.ppermute(g_now[-1] if g_now else u_in, axis_name=along_axis, perm=blocks_here)
+            g_now.append(z)
+        else:
+            later = lax.ppermute(z2[-1] if z2 else u_in, along_axis, perm=by_rank)
+            z2.append(later)
+    r_now = jnp.stack([*g_now[::-1], u_in, *z2], 0)
+    all_values = lax.axis_index(along_axis)
+    latest = all_values - len(g_now)
+    r_now = r_now[(jnp.arange(num) - latest) % num]
+    return _define_terms(r_now, out_dim)
 
 
 def local(
@@ -46,7 +71,7 @@
     third_end = second_end + widths[2]
     whole = lax.all_gather(normed, "mdl", axis=0, tiled=True)
     packed = jnp.concatenate((gate_proj, value_proj, state_proj, step_proj), 1)
-    joined_piece = lax.all_gather(packed, "req", axis=0, tiled=True)
+    joined_piece = write_object(packed, 0, "req")
     joined = jnp.dot(whole, joined_piece, preferred_element_type=jnp.float32)
     gates = joined[:, :first_end].astype(jnp.bfloat16)
     values = joined[:, first_end:second_end].astype(jnp.bfloat16)

time: 202 us -> 252 us (1.25)
  starting transfers between devices: 6.91 us -> 77.5 us
  waiting for transfers between devices: 118 us -> 60.5 us
  local copies, waits for them, and re-layouts: 13.4 us -> 47.3 us
  other arithmetic: 10.6 us -> 13.5 us
    all_gather x1 -> x0, waiting for transfers between devices: 76.5 us -> none  [local(): joined_piece = lax.all_gather(packed, 'req', axis=0, tiled=True)]
    ppermute x0 -> x15, starting transfers between devices: none -> 70.6 us  [the longest x8 62.8 us: write_object(): lax.ppermute(g_now[-1] if g_now else u_in, axis_name=along_axis, perm=blo...]
    ppermute x0 -> x15, waiting for transfers between devices: none -> 49.1 us  [the longest x8 49.1 us: write_object(): lax.ppermute(g_now[-1] if g_now else u_in, axis_name=along_axis, perm=blo...]
    all_gather x1, waiting for transfers between devices: 30.4 us -> 0.02 us  [local(): lax.all_gather(out_proj, 'req', axis=1, tiled=True)]
    unnamed x37 -> x69, local copies, waits for them, and re-layouts: 3.61 us -> 24.5 us
    gather x0 -> x1, local copies, waits for them, and re-layouts: none -> 9.84 us  [write_object(): r_now = r_now[(jnp.arange(num) - latest) % num]]
  transfers between devices with their start and end apart: 5 -> 19, of which waited for: 3 -> 8; matrix products, arithmetic and copies ran while one was open for 17% -> 28% of each run, Pallas kernels for 0% -> 0%
where the time goes in v1:
time: 252 us; the launch traced here: 251 us
  starting transfers between devices  77.5 us (31%)
  waiting for transfers between devices  60.5 us (24%)
  local copies, waits for them, and re-layouts  47.3 us (19%)
  matrix products  21.4 us (8%)
  blocking collectives  16 us (6%)
  between operations  14.6 us (6%)
  other arithmetic  13.5 us (5%)
    ppermute x8, starting transfers between devices, write_object(): lax.ppermute(g_now[-1] if g_now else u_in, axis_name=along_axis, perm=blo...  62.8 us
    ppermute x8, waiting for transfers between devices, write_object(): lax.ppermute(g_now[-1] if g_now else u_in, axis_name=along_axis, perm=blo...  49.1 us
    unnamed x69, local copies, waits for them, and re-layouts  24.5 us
    all_to_all x1, waiting for transfers between devices, local(): lax.all_to_all(state_here.reshape(requests, heads_here, head_dim * nstate...  11.4 us
    all_gather x1, blocking collectives, local(): whole = lax.all_gather(normed, 'mdl', axis=0, tiled=True)  11.1 us
    gather x1, local copies, waits for them, and re-layouts, write_object(): r_now = r_now[(jnp.arange(num) - latest) % num]  9.84 us
    dot_general x1, matrix products, local(): joined = jnp.dot(whole, joined_piece, preferred_element_type=jnp.float32)  8.28 us
    ppermute x7, starting transfers between devices, write_object(): later = lax.ppermute(z2[-1] if z2 else u_in, along_axis, perm=by_rank)  7.86 us
  transfers between devices with their start and end apart: 19, of which 8 were waited for; matrix products, arithmetic and copies ran while one was open for 28% of the time, Pallas kernels for 0%

profile of v1, /device:TPU:0, one launch (start us, length us, event | category | flops | bytes accessed | tf_op | source)
XLA Modules:
  0.0 250.8 jit_solution(1904856078289133528)
XLA Ops:
  8.2 1.1 pad_maximum_fusion
  9.8 13.3 %collective-permute-done = bf16[96,3352]{1,0:T(8,128)(2,1)S(1)} collective-permute-done((bf16[96,3352]{1,0:T(8,128)(2,1)S(1)}, bf16[96,3352]{1,0:T(8,128)(2,1)S(1)}, u32[]{:S(2)}, u32[]{:S(2)}) %collective-permute-start) | collective-permute-done | bytes 643616 | tf_op jit(solution)/shard_map/ppermute | solution.py:23
  23.1 4.4 %collective-permute-start.8 = (bf16[96,3352]{1,0:T(8,128)(2,1)S(1)}, bf16[96,3352]{1,0:T(8,128)(2,1)S(1)}, u32[]{:S(2)}, u32[]{:S(2)}) collective-permute-start(bf16[96,3352]{1,0:T(8,128)(2,1)S(1)} %pad_maximum_fusion), channel_id=1, source_target_pairs={{2,0},{4,2},{6,4},{8,6},{10,8},{12,10},{14,12},{16,14},{18,16},{20... | collective-permute-start | bytes 1930760 | tf_op jit(solution)/shard_map/ppermute | solution.py:26
  27.6 8.5 %collective-permute-done.1 = bf16[96,3352]{1,0:T(8,128)(2,1)S(1)} collective-permute-done((bf16[96,3352]{1,0:T(8,128)(2,1)S(1)}, bf16[96,3352]{1,0:T(8,128)(2,1)S(1)}, u32[]{:S(2)}, u32[]{:S(2)}) %collective-permute-start.1) | collective-permute-done | bytes 643616 | tf_op jit(solution)/shard_map/ppermute | solution.py:23
  36.0 1.2 collective-permute-start.2
  37.2 3.2 %collective-permute-start.9 = (bf16[96,3352]{1,0:T(8,128)(2,1)S(1)}, bf16[96,3352]{1,0:T(8,128)(2,1)S(1)}, u32[]{:S(2)}, u32[]{:S(2)}) collective-permute-start(bf16[96,3352]{1,0:T(8,128)(2,1)S(1)} %collective-permute-done.8), channel_id=1, source_target_pairs={{2,0},{4,2},{6,4},{8,6},{10,8},{12,10},{14,12},{16,14},{18,16},{20... | collective-permute-start | bytes 1930760 | tf_op jit(solution)/shard_map/ppermute | solution.py:26
  40.5 8.6 %collective-permute-done.2 = bf16[96,3352]{1,0:T(8,128)(2,1)} collective-permute-done((bf16[96,3352]{1,0:T(8,128)(2,1)S(1)}, bf16[96,3352]{1,0:T(8,128)(2,1)}, u32[]{:S(2)}, u32[]{:S(2)}) %collective-permute-start.2) | collective-permute-done | bytes 643616 | tf_op jit(solution)/shard_map/ppermute | solution.py:23
  49.0 4.6 %collective-permute-start.3 = (bf16[96,3352]{1,0:T(8,128)(2,1)}, bf16[96,3352]{1,0:T(8,128)(2,1)}, u32[]{:S(2)}, u32[]{:S(2)}) collective-permute-start(bf16[96,3352]{1,0:T(8,128)(2,1)} %collective-permute-done.2), channel_id=1, source_target_pairs={{0,2},{2,4},{4,6},{6,8},{8,10},{10,12},{12,14},{14,16},{16,18},{18... | collective-permute-start | bytes 1930760 | tf_op jit(solution)/shard_map/ppermute | solution.py:23
  53.7 1.2 dynamic_slice.10
  55.1 7.2 %collective-permute-done.3 = bf16[96,3352]{1,0:T(8,128)(2,1)} collective-permute-done((bf16[96,3352]{1,0:T(8,128)(2,1)}, bf16[96,3352]{1,0:T(8,128)(2,1)}, u32[]{:S(2)}, u32[]{:S(2)}) %collective-permute-start.3) | collective-permute-done | bytes 643616 | tf_op jit(solution)/shard_map/ppermute | solution.py:23
  62.2 12.2 %collective-permute-start.4 = (bf16[96,3352]{1,0:T(8,128)(2,1)}, bf16[96,3352]{1,0:T(8,128)(2,1)S(1)}, u32[]{:S(2)}, u32[]{:S(2)}) collective-permute-start(bf16[96,3352]{1,0:T(8,128)(2,1)} %collective-permute-done.3), channel_id=1, source_target_pairs={{0,2},{2,4},{4,6},{6,8},{8,10},{10,12},{12,14},{14,16},{16,18},{18... | collective-permute-start | bytes 1930760 | tf_op jit(solution)/shard_map/ppermute | solution.py:23
  77.6 6.5 %collective-permute-done.4 = bf16[96,3352]{1,0:T(8,128)(2,1)S(1)} collective-permute-done((bf16[96,3352]{1,0:T(8,128)(2,1)}, bf16[96,3352]{1,0:T(8,128)(2,1)S(1)}, u32[]{:S(2)}, u32[]{:S(2)}) %collective-permute-start.4) | collective-permute-done | bytes 643616 | tf_op jit(solution)/shard_map/ppermute | solution.py:23
  84.1 13.1 %collective-permute-start.5 = (bf16[96,3352]{1,0:T(8,128)(2,1)S(1)}, bf16[96,3352]{1,0:T(8,128)(2,1)}, u32[]{:S(2)}, u32[]{:S(2)}) collective-permute-start(bf16[96,3352]{1,0:T(8,128)(2,1)S(1)} %collective-permute-done.4), channel_id=1, source_target_pairs={{0,2},{2,4},{4,6},{6,8},{8,10},{10,12},{12,14},{14,16},{16,18},{18... | collective-permute-start | bytes 1930760 | tf_op jit(solution)/shard_map/ppermute | solution.py:23
  97.9 5.0 %collective-permute-done.5 = bf16[96,3352]{1,0:T(8,128)(2,1)} collective-permute-done((bf16[96,3352]{1,0:T(8,128)(2,1)S(1)}, bf16[96,3352]{1,0:T(8,128)(2,1)}, u32[]{:S(2)}, u32[]{:S(2)}) %collective-permute-start.5) | collective-permute-done | bytes 643616 | tf_op jit(solution)/shard_map/ppermute | solution.py:23
  102.9 15.9 %collective-permute-start.6 = (bf16[96,3352]{1,0:T(8,128)(2,1)}, bf16[96,3352]{1,0:T(8,128)(2,1)}, u32[]{:S(2)}, u32[]{:S(2)}) collective-permute-start(bf16[96,3352]{1,0:T(8,128)(2,1)} %collective-permute-done.5), channel_id=1, source_target_pairs={{0,2},{2,4},{4,6},{6,8},{8,10},{10,12},{12,14},{14,16},{16,18},{18... | collective-permute-start | bytes 1930760 | tf_op jit(solution)/shard_map/ppermute | solution.py:23
  118.7 1.2 compare_convert_fusion.1
  121.1 15.3 %collective-permute-start.7 = (bf16[96,3352]{1,0:T(8,128)(2,1)}, bf16[96,3352]{1,0:T(8,128)(2,1)S(1)}, u32[]{:S(2)}, u32[]{:S(2)}) collective-permute-start(bf16[96,3352]{1,0:T(8,128)(2,1)} %collective-permute-done.6), channel_id=1, source_target_pairs={{0,2},{2,4},{4,6},{6,8},{8,10},{10,12},{12,14},{14,16},{16,18},{18... | collective-permute-start | bytes 1930760 | tf_op jit(solution)/shard_map/ppermute | solution.py:23
  136.4 11.1 %all_gather.6 = bf16[256,1536]{1,0:T(8,128)(2,1)S(1)} all-gather(bf16[128,1536]{1,0:T(8,128)(2,1)S(1)} %fusion.26), channel_id=1, replica_groups=mesh['req'=16,'mdl'=2] {'mdl'}, dimensions={0}, use_global_device_ids=true | all-gather | bytes 1179648 | tf_op jit(solution)/shard_map/all_gather | solution.py:72
  148.8 0.9 bitcast_dynamic-update-slice_fusion.15
  149.7 2.0 bitcast_dynamic-update-slice_fusion.14
  151.7 2.0 bitcast_dynamic-update-slice_fusion.13
  154.6 2.0 bitcast_dynamic-update-slice_fusion.11
  156.5 2.0 bitcast_dynamic-update-slice_fusion.10
  160.4 0.9 bitcast_dynamic-update-slice_fusion.7
  163.1 0.9 bitcast_dynamic-update-slice_fusion.4
  164.0 2.0 bitcast_dynamic-update-slice_fusion.3
  166.0 2.0 bitcast_dynamic-update-slice_fusion.2
  168.9 0.9 bitcast_dynamic-update-slice_fusion
  169.8 9.8 %gather_fusion = bf16[16,96,3352]{2,1,0:T(8,128)(2,1)} fusion(bf16[16,96,3352]{2,1,0:T(8,128)(2,1)} %bitcast_dynamic-update-slice_fusion, s32[1024]{0:T(1024)} %pad_clamp_fusion), kind=kCustom, calls=%fused_computation | custom fusion | bytes 20594752 | tf_op jit(solution)/shard_map/gather | solution.py:31
  179.7 8.3 %convolution_convert_fusion = bf16[256,3352]{0,1:T(8,128)(2,1)S(1)} fusion(bf16[256,1536]{1,0:T(8,128)(2,1)S(1)} %all_gather.6, bf16[1536,3352]{1,0:T(8,128)(2,1)} %bitcast.106), kind=kOutput, calls=%fused_computation.2 | convolution fusion | flops 2636978176 | bytes 12800000 | tf_op jit(solution)/shard_map/dot_general | solution.py:75
  188.0 1.2 copy-done.3
  190.3 1.0 copy.57
  191.9 1.2 multiply_convert_fusion
  193.1 0.9 slice.92
  194.1 2.5 copy.54
  197.4 1.1 multiply_reduce_fusion.1
  200.3 3.5 %fusion.10 = f32[2,128,24,64]{1,3,2,0:T(8,128)S(1)} fusion(bf16[2,128,24,64]{1,3,2,0:T(8,128)(2,1)S(1)} %bitcast.111, f32[2,128,24,64]{1,3,2,0:T(8,128)S(1)} %fusion.30, f32[2,128,24]{1,2,0:T(8,128)S(1)} %compare_select_fusion, f32[2,128,24]{1,2,0:T(8,128)S(1)} %get-tuple-element.13, f32[2,128,128]{2,1,0:T(8,128)S(1)} %fusion.34, ...), kind=kOutput, calls=%fused_computation.23 | convolution fusion | flops 609091584 | bytes 4153440 | tf_op jit(solution)/shard_map/gtsh,gshp->gthp/dot_general | solution.py:108
  203.9 1.2 copy.56
  205.2 5.3 %convolution_convert_fusion.1 = bf16[256,1536]{1,0:T(8,128)(2,1)} fusion(bf16[1536,1536]{0,1:T(8,128)(2,1)} %all-gather.2.cloned.1.call-done, f32[1536]{0:T(1024)S(1)} %copy-done.20, f32[192,8,2,128]{3,2,1,0:T(2,128)S(1)} %bitcast.107, bf16[256,3352]{0,1:T(8,128)(2,1)} %copy-done.3), kind=kOutput, calls=%fused_computation.9 | convolution fusion | flops 1211498496 | bytes 7870464 | tf_op jit(solution)/shard_map/dot_general | solution.py:118
  211.5 3.2 %all-to-all-start.1 = ((bf16[2,24,192]{2,1,0:T(8,128)(2,1)}), bf16[2,24,192]{2,1,0:T(8,128)(2,1)S(1)}, u32[]{:S(2)}, u32[]{:S(2)}) async-start(bf16[2,24,192]{2,1,0:T(8,128)(2,1)} %convert_element_type.123), calls=%async_computation.2 | async-start | bytes 49152 | tf_op jit(solution)/shard_map/all_to_all | solution.py:154
  214.7 1.7 multiply_reduce_fusion
  216.4 4.9 %psum.7 = f32[256]{0:T(256)S(1)} all-reduce(f32[256]{0:T(256)S(1)} %multiply_reduce_fusion), channel_id=1, replica_groups=mesh['req'=16,'mdl'=2] {'mdl'}, use_global_device_ids=true, to_apply=%region_3.4 | all-reduce | flops 256 | bytes 2048 | tf_op jit(solution)/shard_map/psum | solution.py:116
  221.3 2.2 add_convert_fusion
  223.6 1.2 convert_element_type.118
  224.9 3.5 %all-to-all-start = ((bf16[2,24,8192]{2,1,0:T(8,128)(2,1)}), bf16[2,24,8192]{2,1,0:T(8,128)(2,1)S(1)}, u32[]{:S(2)}, u32[]{:S(2)}) async-start(bf16[2,24,8192]{2,1,0:T(8,128)(2,1)} %convert_element_type.118), calls=%async_computation.1 | async-start | bytes 1572864 | tf_op jit(solution)/shard_map/all_to_all | solution.py:147
  229.2 11.4 %all-to-all-done = bf16[2,24,8192]{2,1,0:T(8,128)(2,1)S(1)} async-done(((bf16[2,24,8192]{2,1,0:T(8,128)(2,1)}), bf16[2,24,8192]{2,1,0:T(8,128)(2,1)S(1)}, u32[]{:S(2)}, u32[]{:S(2)}) %all-to-all-start) | async-done | bytes 786464 | tf_op jit(solution)/shard_map/all_to_all | solution.py:147
  240.6 1.3 copy.66
  242.0 2.0 multiply_convert_fusion.3
  (120 shorter events, 19.4 us)
Async XLA Ops:
  7.2 69.4 %copy-start.4 = (bf16[128,1536]{1,0:T(8,128)(2,1)S(1)}, bf16[128,1536]{1,0:T(8,128)(2,1)}, u32[]{:S(2)}) copy-start(bf16[128,1536]{1,0:T(8,128)(2,1)} %param.18) | copy-start | bytes 1179652
  7.2 90.0 %copy-start.22 = (s32[2]{0:T(128)S(1)}, s32[2]{0:T(128)}, u32[]{:S(2)}) copy-start(s32[2]{0:T(128)} %param.35) | copy-start | bytes 28
  7.2 112.8 %copy-start.12 = (bf16[2,3,1536]{2,0,1:T(2,128)(2,1)S(1)}, bf16[2,3,1536]{2,0,1:T(2,128)(2,1)}, u32[]{:S(2)}) copy-start(bf16[2,3,1536]{2,0,1:T(2,128)(2,1)} %param.32) | copy-start | bytes 55300
  7.2 112.8 %copy-start.14 = (bf16[2,3,256]{2,0,1:T(2,128)(2,1)S(1)}, bf16[2,3,256]{2,0,1:T(2,128)(2,1)}, u32[]{:S(2)}) copy-start(bf16[2,3,256]{2,0,1:T(2,128)(2,1)} %param.33) | copy-start | bytes 9220
  7.2 112.9 %copy-start.21 = (f32[24]{0:T(128)S(1)}, f32[24]{0:T(128)}, u32[]{:S(2)}) copy-start(f32[24]{0:T(128)} %param.27) | copy-start | bytes 292
  7.2 113.5 %copy-start.13 = (f32[1536]{0:T(1024)S(1)}, f32[1536]{0:T(1024)}, u32[]{:S(2)}) copy-start(f32[1536]{0:T(1024)} %param.19) | copy-start | bytes 18436
  7.2 197.9 %all-gather.2.cloned.1.call-start = ((), (), s32[]{:S(2)}) async-start(), calls=%async_computation.3 | async-start | bytes 5013504 | tf_op jit(solution)/shard_map/all_gather | solution.py:120
  9.3 13.8 %collective-permute-start = (bf16[96,3352]{1,0:T(8,128)(2,1)S(1)}, bf16[96,3352]{1,0:T(8,128)(2,1)S(1)}, u32[]{:S(2)}, u32[]{:S(2)}) collective-permute-start(bf16[96,3352]{1,0:T(8,128)(2,1)S(1)} %pad_maximum_fusion), channel_id=1, source_target_pairs={{0,2},{2,4},{4,6},{6,8},{8,10},{10,12},{12,14},{14,16},{16,18},{18... | collective-permute-start | bytes 1930760 | tf_op jit(solution)/shard_map/ppermute | solution.py:23
  23.1 12.9 %collective-permute-start.1 = (bf16[96,3352]{1,0:T(8,128)(2,1)S(1)}, bf16[96,3352]{1,0:T(8,128)(2,1)S(1)}, u32[]{:S(2)}, u32[]{:S(2)}) collective-permute-start(bf16[96,3352]{1,0:T(8,128)(2,1)S(1)} %collective-permute-done), channel_id=1, source_target_pairs={{0,2},{2,4},{4,6},{6,8},{8,10},{10,12},{12,14},{14,16},{16,18},{18... | collective-permute-start | bytes 1930760 | tf_op jit(solution)/shard_map/ppermute | solution.py:23
  23.1 14.1 %collective-permute-start.8 = (bf16[96,3352]{1,0:T(8,128)(2,1)S(1)}, bf16[96,3352]{1,0:T(8,128)(2,1)S(1)}, u32[]{:S(2)}, u32[]{:S(2)}) collective-permute-start(bf16[96,3352]{1,0:T(8,128)(2,1)S(1)} %pad_maximum_fusion), channel_id=1, source_target_pairs={{2,0},{4,2},{6,4},{8,6},{10,8},{12,10},{14,12},{16,14},{18,16},{20... | collective-permute-start | bytes 1930760 | tf_op jit(solution)/shard_map/ppermute | solution.py:26
  36.0 13.0 %collective-permute-start.2 = (bf16[96,3352]{1,0:T(8,128)(2,1)S(1)}, bf16[96,3352]{1,0:T(8,128)(2,1)}, u32[]{:S(2)}, u32[]{:S(2)}) collective-permute-start(bf16[96,3352]{1,0:T(8,128)(2,1)S(1)} %collective-permute-done.1), channel_id=1, source_target_pairs={{0,2},{2,4},{4,6},{6,8},{8,10},{10,12},{12,14},{14,16},{16,18},{18... | collective-permute-start | bytes 1930760 | tf_op jit(solution)/shard_map/ppermute | solution.py:23
  37.2 17.8 %collective-permute-start.9 = (bf16[96,3352]{1,0:T(8,128)(2,1)S(1)}, bf16[96,3352]{1,0:T(8,128)(2,1)S(1)}, u32[]{:S(2)}, u32[]{:S(2)}) collective-permute-start(bf16[96,3352]{1,0:T(8,128)(2,1)S(1)} %collective-permute-done.8), channel_id=1, source_target_pairs={{2,0},{4,2},{6,4},{8,6},{10,8},{12,10},{14,12},{16,14},{18,16},{20... | collective-permute-start | bytes 1930760 | tf_op jit(solution)/shard_map/ppermute | solution.py:26
  49.0 13.2 %collective-permute-start.3 = (bf16[96,3352]{1,0:T(8,128)(2,1)}, bf16[96,3352]{1,0:T(8,128)(2,1)}, u32[]{:S(2)}, u32[]{:S(2)}) collective-permute-start(bf16[96,3352]{1,0:T(8,128)(2,1)} %collective-permute-done.2), channel_id=1, source_target_pairs={{0,2},{2,4},{4,6},{6,8},{8,10},{10,12},{12,14},{14,16},{16,18},{18... | collective-permute-start | bytes 1930760 | tf_op jit(solution)/shard_map/ppermute | solution.py:23
  53.7 188.3 %reduce-scatter.2.cloned.1.call-start = ((), (), s32[]{:S(2)}) async-start(), calls=%async_computation.4 | async-start | bytes 1179648 | tf_op jit(solution)/shard_map/reduce_scatter | solution.py:123
  55.0 21.7 %collective-permute-start.10 = (bf16[96,3352]{1,0:T(8,128)(2,1)S(1)}, bf16[96,3352]{1,0:T(8,128)(2,1)S(1)}, u32[]{:S(2)}, u32[]{:S(2)}) collective-permute-start(bf16[96,3352]{1,0:T(8,128)(2,1)S(1)} %collective-permute-done.9), channel_id=1, source_target_pairs={{2,0},{4,2},{6,4},{8,6},{10,8},{12,10},{14,12},{16,14},{18,16},{20... | collective-permute-start | bytes 1930760 | tf_op jit(solution)/shard_map/ppermute | solution.py:26
  62.2 21.9 %collective-permute-start.4 = (bf16[96,3352]{1,0:T(8,128)(2,1)}, bf16[96,3352]{1,0:T(8,128)(2,1)S(1)}, u32[]{:S(2)}, u32[]{:S(2)}) collective-permute-start(bf16[96,3352]{1,0:T(8,128)(2,1)} %collective-permute-done.3), channel_id=1, source_target_pairs={{0,2},{2,4},{4,6},{6,8},{8,10},{10,12},{12,14},{14,16},{16,18},{18... | collective-permute-start | bytes 1930760 | tf_op jit(solution)/shard_map/ppermute | solution.py:23
  76.7 0.8 copy-start.7
  77.6 20.2 %collective-permute-start.11 = (bf16[96,3352]{1,0:T(8,128)(2,1)S(1)}, bf16[96,3352]{1,0:T(8,128)(2,1)}, u32[]{:S(2)}, u32[]{:S(2)}) collective-permute-start(bf16[96,3352]{1,0:T(8,128)(2,1)S(1)} %collective-permute-done.10), channel_id=1, source_target_pairs={{2,0},{4,2},{6,4},{8,6},{10,8},{12,10},{14,12},{16,14},{18,16},{20... | collective-permute-start | bytes 1930760 | tf_op jit(solution)/shard_map/ppermute | solution.py:26
  84.1 13.7 %copy-start.9 = (bf16[96,3352]{1,0:T(8,128)(2,1)}, bf16[96,3352]{1,0:T(8,128)(2,1)S(1)}, u32[]{:S(2)}) copy-start(bf16[96,3352]{1,0:T(8,128)(2,1)S(1)} %collective-permute-done.4) | copy-start | bytes 1930756
  84.1 18.8 %collective-permute-start.5 = (bf16[96,3352]{1,0:T(8,128)(2,1)S(1)}, bf16[96,3352]{1,0:T(8,128)(2,1)}, u32[]{:S(2)}, u32[]{:S(2)}) collective-permute-start(bf16[96,3352]{1,0:T(8,128)(2,1)S(1)} %collective-permute-done.4), channel_id=1, source_target_pairs={{0,2},{2,4},{4,6},{6,8},{8,10},{10,12},{12,14},{14,16},{16,18},{18... | collective-permute-start | bytes 1930760 | tf_op jit(solution)/shard_map/ppermute | solution.py:23
  97.8 23.1 %collective-permute-start.12 = (bf16[96,3352]{1,0:T(8,128)(2,1)}, bf16[96,3352]{1,0:T(8,128)(2,1)}, u32[]{:S(2)}, u32[]{:S(2)}) collective-permute-start(bf16[96,3352]{1,0:T(8,128)(2,1)} %collective-permute-done.11), channel_id=1, source_target_pairs={{2,0},{4,2},{6,4},{8,6},{10,8},{12,10},{14,12},{16,14},{18,16},{20... | collective-permute-start | bytes 1930760 | tf_op jit(solution)/shard_map/ppermute | solution.py:26
  102.9 18.2 %collective-permute-start.6 = (bf16[96,3352]{1,0:T(8,128)(2,1)}, bf16[96,3352]{1,0:T(8,128)(2,1)}, u32[]{:S(2)}, u32[]{:S(2)}) collective-permute-start(bf16[96,3352]{1,0:T(8,128)(2,1)} %collective-permute-done.5), channel_id=1, source_target_pairs={{0,2},{2,4},{4,6},{6,8},{8,10},{10,12},{12,14},{14,16},{16,18},{18... | collective-permute-start | bytes 1930760 | tf_op jit(solution)/shard_map/ppermute | solution.py:23
  120.9 27.8 %collective-permute-start.13 = (bf16[96,3352]{1,0:T(8,128)(2,1)}, bf16[96,3352]{1,0:T(8,128)(2,1)S(1)}, u32[]{:S(2)}, u32[]{:S(2)}) collective-permute-start(bf16[96,3352]{1,0:T(8,128)(2,1)} %collective-permute-done.12), channel_id=1, source_target_pairs={{2,0},{4,2},{6,4},{8,6},{10,8},{12,10},{14,12},{16,14},{18,16},{20... | collective-permute-start | bytes 1930760 | tf_op jit(solution)/shard_map/ppermute | solution.py:26
  121.1 27.7 %collective-permute-start.7 = (bf16[96,3352]{1,0:T(8,128)(2,1)}, bf16[96,3352]{1,0:T(8,128)(2,1)S(1)}, u32[]{:S(2)}, u32[]{:S(2)}) collective-permute-start(bf16[96,3352]{1,0:T(8,128)(2,1)} %collective-permute-done.6), channel_id=1, source_target_pairs={{0,2},{2,4},{4,6},{6,8},{8,10},{10,12},{12,14},{14,16},{16,18},{18... | collective-permute-start | bytes 1930760 | tf_op jit(solution)/shard_map/ppermute | solution.py:23
  148.7 4.9 %copy-start.10 = (bf16[96,3352]{1,0:T(8,128)(2,1)S(1)}, bf16[96,3352]{1,0:T(8,128)(2,1)}, u32[]{:S(2)}) copy-start(bf16[96,3352]{1,0:T(8,128)(2,1)} %copy-done.9) | copy-start | bytes 1930756
  148.7 20.2 %collective-permute-start.14 = (bf16[96,3352]{1,0:T(8,128)(2,1)S(1)}, bf16[96,3352]{1,0:T(8,128)(2,1)S(1)}, u32[]{:S(2)}, u32[]{:S(2)}) collective-permute-start(bf16[96,3352]{1,0:T(8,128)(2,1)S(1)} %collective-permute-done.13), channel_id=1, source_target_pairs={{2,0},{4,2},{6,4},{8,6},{10,8},{12,10},{14,12},{16,14},{18,16},{20... | collective-permute-start | bytes 1930760 | tf_op jit(solution)/shard_map/ppermute | solution.py:26
  156.5 3.8 %copy-start.5 = (bf16[96,1536]{1,0:T(8,128)(2,1)S(1)}, bf16[96,1536]{1,0:T(8,128)(2,1)}, u32[]{:S(2)}) copy-start(bf16[96,1536]{1,0:T(8,128)(2,1)} %param.21) | copy-start | bytes 884740
  156.5 3.8 %copy-start.6 = (bf16[96,1536]{1,0:T(8,128)(2,1)S(1)}, bf16[96,1536]{1,0:T(8,128)(2,1)}, u32[]{:S(2)}) copy-start(bf16[96,1536]{1,0:T(8,128)(2,1)} %param.20) | copy-start | bytes 884740
  156.5 3.8 %copy-start.11 = (bf16[96,256]{1,0:T(8,128)(2,1)S(1)}, bf16[96,256]{1,0:T(8,128)(2,1)}, u32[]{:S(2)}) copy-start(bf16[96,256]{1,0:T(8,128)(2,1)} %param.22) | copy-start | bytes 147460
  160.4 2.7 %copy-start.8 = (bf16[96,3352]{1,0:T(8,128)(2,1)S(1)}, bf16[96,3352]{1,0:T(8,128)(2,1)}, u32[]{:S(2)}) copy-start(bf16[96,3352]{1,0:T(8,128)(2,1)} %copy-done.7) | copy-start | bytes 1930756
  188.0 1.2 copy-start.3
  193.1 6.4 %copy-start.1 = (bf16[2,128,1792]{2,1,0:T(8,128)(2,1)}, bf16[2,128,1792]{2,1,0:T(8,128)(2,1)S(1)}, u32[]{:S(2)}) copy-start(bf16[2,128,1792]{2,1,0:T(8,128)(2,1)S(1)} %multiply_convert_fusion) | copy-start | bytes 2752516
  193.1 3.4 %copy-start.15 = (f32[24]{0:T(128)S(1)}, f32[24]{0:T(128)}, u32[]{:S(2)}) copy-start(f32[24]{0:T(128)} %param.26) | copy-start | bytes 292
  193.1 4.2 %copy-start.17 = (f32[2,128]{1,0:T(2,128)S(1)}, f32[2,128]{1,0:T(2,128)}, u32[]{:S(2)}) copy-start(f32[2,128]{1,0:T(2,128)} %get-tuple-element.11) | copy-start | bytes 3076
  193.1 4.2 %copy-start.24 = (f32[24]{0:T(128)S(1)}, f32[24]{0:T(128)}, u32[]{:S(2)}) copy-start(f32[24]{0:T(128)} %exp.37) | copy-start | bytes 292
  193.1 5.4 %copy-start.16 = (pred[2,128]{1,0:T(4,128)(4,1)S(1)}, pred[2,128]{1,0:T(4,128)(4,1)}, u32[]{:S(2)}) copy-start(pred[2,128]{1,0:T(4,128)(4,1)} %get-tuple-element.10) | copy-start | bytes 772
  193.1 6.3 %copy-start = (f32[2,24,64,128]{3,2,1,0:T(8,128)S(1)}, f32[2,24,64,128]{3,2,1,0:T(8,128)}, u32[]{:S(2)}) copy-start(f32[2,24,64,128]{3,2,1,0:T(8,128)} %param.31) | copy-start | bytes 4718596
  197.3 3.0 %copy-start.2 = (bf16[2,128,1536]{1,2,0:T(8,128)(2,1)S(1)}, bf16[2,128,1536]{1,2,0:T(8,128)(2,1)}, u32[]{:S(2)}) copy-start(bf16[2,128,1536]{1,2,0:T(8,128)(2,1)} %copy.54) | copy-start | bytes 2359300
  197.4 3.0 %copy-start.23 = (f32[24]{0:T(128)S(1)}, f32[24]{0:T(128)}, u32[]{:S(2)}) copy-start(f32[24]{0:T(128)} %param.28) | copy-start | bytes 292
  203.9 1.3 copy-start.20
  205.2 5.3 %copy-start.19 = (pred[2,3]{1,0:T(4,128)(4,1)S(1)}, pred[2,3]{1,0:T(4,128)(4,1)}, u32[]{:S(2)}) copy-start(pred[2,3]{1,0:T(4,128)(4,1)} %compare_and_fusion) | copy-start | bytes 22
  211.5 13.4 %all-to-all-start.1 = ((bf16[2,24,192]{2,1,0:T(8,128)(2,1)}), bf16[2,24,192]{2,1,0:T(8,128)(2,1)S(1)}, u32[]{:S(2)}, u32[]{:S(2)}) async-start(bf16[2,24,192]{2,1,0:T(8,128)(2,1)} %convert_element_type.123), calls=%async_computation.2 | async-start | bytes 49152 | tf_op jit(solution)/shard_map/all_to_all | solution.py:154
  224.9 17.1 %copy-start.18 = (f32[128]{0:T(128)S(1)}, f32[128]{0:T(128)}, u32[]{:S(2)}) copy-start(f32[128]{0:T(128)} %compare_convert_fusion.1) | copy-start | bytes 1540
  224.9 15.8 %all-to-all-start = ((bf16[2,24,8192]{2,1,0:T(8,128)(2,1)}), bf16[2,24,8192]{2,1,0:T(8,128)(2,1)S(1)}, u32[]{:S(2)}, u32[]{:S(2)}) async-start(bf16[2,24,8192]{2,1,0:T(8,128)(2,1)} %convert_element_type.118), calls=%async_computation.1 | async-start | bytes 1572864 | tf_op jit(solution)/shard_map/all_to_all | solution.py:147
Sparse Core Ops, SparseCore 0:
  53.8 79.0 all-gather.1
  210.6 23.2 reduce-scatter.1
